TPU v7x, 256 devices: a whole 4x4x8 slice. The times are simulated.
256 devices in a mesh: outer: 4 (over y), inner: 64 (over z, x, core).
Axes of the slice: x: 4, y: 4, z: 8, core: 2. Of those that a mesh axis runs over, the one named last changes fastest.
Arguments:
- inputs: bfloat16 [2, 16384, 4096], P(None, ('outer', 'inner')), may hold values from -6 to 6
- grad_out: bfloat16 [2, 16384, 4096], P(None, ('outer', 'inner')), may hold values from -6 to 6
- gate_weights: bfloat16 [2, 16, 256, 256], replicated, may hold values from -0.375 to 0.375
- gate_biases: float32 [2, 4096], replicated, may hold values from -4 to 4
- decay_rate: float32 [4096], replicated, may hold values from 1.2207031e-06 to 0.00833333333, as said below
Outputs:
- input_grad: bfloat16 [2, 16384, 4096], P(None, ('outer', 'inner'))
- gate_grads: float32 [8192, 256], P(('outer', 'inner'))
- bias_grads: float32 [2, 4096], replicated
- rate_grad: float32 [4096], replicated
Inputs may be any that keep to these rules, and one draw needn't show every extreme that they name: `decay_rate`: positive per-channel rates.
All inputs are finite; a program needn't handle non-finite values.
Results may differ from a plain program's by a relative error of at most 0.0025.
Values sent between devices are 32-bit elements; how exact they have to be, the bound alone decides.
A program may use at most 128 MiB of HBM per device.

v0:
```python
import jax
import jax.numpy as jnp
from jax import lax
from jax.sharding import PartitionSpec as P

rate_gain = 8.0


def prefix(value, axis, join, neutral, backward):
    count, mine = (lax.axis_size(axis), lax.axis_index(axis))
    pieces = jax.tree.map(lambda part: lax.all_gather(part, axis), value)
    if backward:
        pieces = jax.tree.map(lambda part: part[::-1], pieces)
        mine = count - 1 - mine
    running = jax.tree.map(
        lambda part, zero: jnp.full_like(part, 0) + jnp.asarray(zero, part.dtype), value, neutral
    )

    def lap(position, running):
        longer = join(running, jax.tree.map(lambda part: part[position], pieces))
        return jax.tree.map(lambda new, old: jnp.where(position < mine, new, old), longer, running)

    return lax.fori_loop(0, count - 1, lap, running)


def compose(earlier, latter):
    return (latter[0] * earlier[0], latter[0] * earlier[1] + latter[1])


def along_time(matrix, array):
    return jnp.einsum("ts,nsd->ntd", matrix, array, precision=lax.Precision.HIGHEST)


def per_device(inputs, grad_out, gate_weights, gate_biases, decay_rate):
    seq_count, step_count, channels = inputs.shape
    blocks = gate_weights.shape[1]
    block_width = gate_weights.shape[2]
    row_count = seq_count * step_count
    pieces = inputs.reshape(row_count, blocks, block_width)
    preacts = jnp.einsum("nkc,gkce->gnke", pieces, gate_weights, preferred_element_type=jnp.float32)
    preacts = preacts.reshape(2, seq_count, step_count, channels) + gate_biases[:, None, None, :]
    recurrence = jax.nn.sigmoid(preacts[0])
    inject = jax.nn.sigmoid(preacts[1])
    values = inputs.astype(jnp.float32)
    log_decay = -rate_gain * recurrence * decay_rate
    decays = jnp.exp(log_decay)
    scales = jnp.sqrt(-jnp.expm1(2.0 * log_decay))
    driven = inject * values
    row_pos = lax.broadcasted_iota(jnp.int32, (step_count, step_count), 0)
    col_pos = lax.broadcasted_iota(jnp.int32, (step_count, step_count), 1)
    lower_incl = (col_pos <= row_pos).astype(jnp.float32)
    lower_strict = (col_pos < row_pos).astype(jnp.float32)
    upper_incl = (col_pos >= row_pos).astype(jnp.float32)
    log_cum = along_time(lower_incl, log_decay)
    cum_mult = jnp.exp(log_cum)
    inverse_mult = jnp.exp(-log_cum)
    scaled_in = scales * driven * inverse_mult
    before_sum = along_time(lower_strict, scaled_in)
    end_mult = cum_mult[:, -1]
    summary = (end_mult, end_mult * (before_sum[:, -1] + scaled_in[:, -1]))
    neutral = (jnp.ones_like(summary[0]), jnp.zeros_like(summary[1]))
    entering = prefix(summary, ("outer", "inner"), compose, neutral, False)[1]
    previous = jnp.exp(log_cum - log_decay) * (entering[:, None] + before_sum)
    upstream = grad_out.astype(jnp.float32)
    tail_sum = along_time(upper_incl, cum_mult * upstream)
    outgoing = (end_mult, tail_sum[:, 0])
    arriving = prefix(outgoing, ("outer", "inner"), compose, neutral, True)[1]
    adjoint = inverse_mult * (tail_sum + (end_mult * arriving)[:, None])
    driven_grad = adjoint * scales
    sensitive = rate_gain * (
        adjoint * driven * decays * decays / scales - adjoint * previous * decays
    )
    pre_recur = decay_rate * sensitive * recurrence * (1.0 - recurrence)
    pre_inject = driven_grad * values * inject * (1.0 - inject)
    rate_part = jnp.sum(recurrence * sensitive, axis=(0, 1))
    bias_part = jnp.stack([jnp.sum(pre_recur, axis=(0, 1)), jnp.sum(pre_inject, axis=(0, 1))])
    pre_grads = jnp.stack([pre_recur, pre_inject]).astype(jnp.bfloat16)
    pre_grads = pre_grads.reshape(2, row_count, blocks, block_width)
    through = jnp.einsum(
        "gnke,gkce->nkc", pre_grads, gate_weights, preferred_element_type=jnp.float32
    )
    input_grad = (driven_grad * inject + through.reshape(seq_count, step_count, channels)).astype(
        jnp.bfloat16
    )
    weight_part = jnp.einsum(
        "nkc,gnke->gkce", pieces, pre_grads, preferred_element_type=jnp.float32
    )
    weight_part = weight_part.reshape(2 * blocks * block_width, block_width)
    gate_grads = lax.psum_scatter(weight_part, ("outer", "inner"), scatter_dimension=0, tiled=True)
    bias_grads, rate_grad = lax.psum((bias_part, rate_part), ("outer", "inner"))
    return (input_grad, gate_grads, bias_grads, rate_grad)


def solution(mesh):
    in_specs = (P(None, ("outer", "inner"), None), P(None, ("outer", "inner"), None), P(), P(), P())
    out_specs = (P(None, ("outer", "inner"), None), P(("outer", "inner"), None), P(), P())
    return jax.shard_map(
        per_device, mesh=mesh, in_specs=in_specs, out_specs=out_specs, check_vma=False
    )
```

profile of v0, /device:TPU:1, one launch (start us, length us, event | category | flops | bytes accessed | tf_op | source)
XLA Modules:
  0.0 2090.9 jit_solution(2075967233272307066)
XLA Ops:
  10.4 5.9 fusion.6
  16.4 5.5 copy.27
  21.9 5.0 reshape.72
  29.6 4.1 multiply_multiply_fusion.1
  37.8 2.8 convolution_bitcast_fusion.1
  42.9 116.6 %all-gather.11.cloned.1.call-done = f32[512,1,4096]{2,1,0:T(1,128)} async-done(((f32[2,1,4096]{2,1,0:T(1,128)}), f32[512,1,4096]{2,1,0:T(1,128)}) %all-gather.11.cloned.1.call-update) | async-done | bytes 8388624 | tf_op jit(solution)/shard_map/all_gather | solution.py:11
  159.5 24.5 %reduce.2 = f32[512,4096]{1,0:T(8,128)} reduce(f32[512,1,4096]{2,1,0:T(1,128)} %all-gather.11.cloned.1.call-done, f32[]{:T(128)} %constant.72), dimensions={1}, to_apply=%all-gather.2.reduce_sub_computation | reduce | bytes 16777220 | tf_op jit(solution)/shard_map/all_gather | solution.py:11
  184.0 10.6 reshape.78
  194.6 84.0 %all-gather.7.cloned.1.call-done = f32[512,1,4096]{2,1,0:T(1,128)} async-done(((f32[2,1,4096]{2,1,0:T(1,128)}), f32[512,1,4096]{2,1,0:T(1,128)}) %all-gather.7.cloned.1.call-update) | async-done | bytes 8388624 | tf_op jit(solution)/shard_map/all_gather | solution.py:11
  278.6 24.5 %reduce = f32[512,4096]{1,0:T(8,128)} reduce(f32[512,1,4096]{2,1,0:T(1,128)} %all-gather.7.cloned.1.call-done, f32[]{:T(128)} %constant.72), dimensions={1}, to_apply=%all-gather.reduce_sub_computation | reduce | bytes 16777220 | tf_op jit(solution)/shard_map/all_gather | solution.py:11
  303.1 10.6 reshape.75
  313.6 215.8 %while.29 = (s32[]{:T(128)}, f32[2,4096]{1,0:T(2,128)S(1)}, s32[]{:T(128)}, f32[256,2,4096]{2,1,0:T(2,128)}, f32[256,2,4096]{2,1,0:T(2,128)}, /*index=5*/s32[]{:T(128)}, s32[]{:T(128)}) while((s32[]{:T(128)}, f32[2,4096]{1,0:T(2,128)S(1)}, s32[]{:T(128)}, f32[256,2,4096]{2,1,0:T(2,128)}, f32[256,2,4096]{2,1,0:T(2,128)}, ...), condition=%wide.region_3.4_spmd.clone, body=%wide.region_2.3_spmd.clone.sunk | while | flops 32772 | bytes 131181 | solution.py:23
  529.5 9.1 rev.6
  538.6 24.5 %reduce.1 = f32[512,4096]{1,0:T(8,128)} reduce(f32[512,1,4096]{2,1,0:T(1,128)} %all-gather.9.cloned.1.call-done, f32[]{:T(128)} %constant.72), dimensions={1}, to_apply=%all-gather.1.reduce_sub_computation | reduce | bytes 16777220 | tf_op jit(solution)/shard_map/all_gather | solution.py:11
  563.1 10.6 reshape.76
  573.7 9.1 rev.7
  582.8 215.8 %while.28 = (s32[]{:T(128)}, f32[2,4096]{1,0:T(2,128)S(1)}, s32[]{:T(128)}, f32[256,2,4096]{2,1,0:T(2,128)}, f32[256,2,4096]{2,1,0:T(2,128)}, /*index=5*/s32[]{:T(128)}, s32[]{:T(128)}) while((s32[]{:T(128)}, f32[2,4096]{1,0:T(2,128)S(1)}, s32[]{:T(128)}, f32[256,2,4096]{2,1,0:T(2,128)}, f32[256,2,4096]{2,1,0:T(2,128)}, ...), condition=%wide.region_1.2_spmd.clone, body=%wide.region_0.1_spmd.clone.sunk | while | flops 32772 | bytes 131181 | solution.py:23
  798.7 7.3 multiply_reduce_fusion
  810.4 3.8 copy.33
  814.2 4.3 fusion.25
  821.1 2.8 reshape.73
  823.9 75.4 %all-reduce = (f32[2,4096]{1,0:T(2,128)}, f32[4096]{0:T(1024)}) all-reduce(f32[2,4096]{1,0:T(2,128)S(1)} %pad_maximum_fusion, f32[4096]{0:T(1024)S(1)} %get-tuple-element.230), channel_id=1, replica_groups=mesh['outer'=4,'inner'=64] {'outer','inner'}, use_global_device_ids=true, to_apply=%region_7.8 | all-reduce | flops 12288 | bytes 98304 | tf_op jit(solution)/shard_map/psum | solution.py:90
  899.3 3.8 add_convert_fusion
  903.1 1181.3 %reduce-scatter.2.cloned.1.call-done = f32[32,256]{1,0:T(8,128)} async-done(((f32[8192,256]{1,0:T(8,128)}), f32[32,256]{1,0:T(8,128)}) %reduce-scatter.2.cloned.1.call-update) | async-done | bytes 32784 | tf_op jit(solution)/shard_map/reduce_scatter | solution.py:89
  (559 shorter events, 441.1 us)
Async XLA Ops:
  7.2 152.4 %all-gather.11.cloned.1.call-start = ((), (), s32[]{:S(2)}) async-start(), calls=%async_computation.4 | async-start | bytes 8421376 | tf_op jit(solution)/shard_map/all_gather | solution.py:11
  10.4 5.9 copy-start.4
  21.9 5.0 copy-start.10
  26.8 2.8 copy-start.3
  29.6 4.1 copy-start
  33.7 4.1 copy-start.8
  35.0 1.3 copy-start.6
  37.0 241.6 %all-gather.7.cloned.1.call-start = ((), (), s32[]{:S(2)}) async-start(), calls=%async_computation.2 | async-start | bytes 8421376 | tf_op jit(solution)/shard_map/all_gather | solution.py:11
  37.8 500.8 %all-gather.9.cloned.1.call-start = ((), (), s32[]{:S(2)}) async-start(), calls=%async_computation.3 | async-start | bytes 8421376 | tf_op jit(solution)/shard_map/all_gather | solution.py:11
  40.7 1.3 copy-start.7
  42.7 2041.7 %reduce-scatter.2.cloned.1.call-start = ((), (), s32[]{:S(2)}) async-start(), calls=%async_computation.1 | async-start | bytes 8421376 | tf_op jit(solution)/shard_map/reduce_scatter | solution.py:89
  573.7 225.0 %copy-start.9 = (f32[2,1,4096]{2,1,0:T(1,128)S(1)}, f32[2,1,4096]{2,1,0:T(1,128)}, u32[]{:S(2)}) copy-start(f32[2,1,4096]{2,1,0:T(1,128)} %get-tuple-element.260) | copy-start | bytes 98308
  798.7 7.3 copy-start.1
  807.8 1.2 copy-start.5
  809.1 1.4 copy-start.2
Sparse Core Ops, SparseCore 0:
  37.2 122.3 all-gather.10
  163.7 114.8 all-gather.6
  282.2 114.8 all-gather.8
  814.4 1269.9 reduce-scatter.1
where the time goes:
time: 2130 us; the launch traced here: 2090 us
  waiting for transfers between devices  1380 us (65%)
  other arithmetic  512 us (24%)
  local copies, waits for them, and re-layouts  77.2 us (4%)
  blocking collectives  75.4 us (4%)
    reduce_scatter x1, waiting for transfers between devices, per_device(): lax.psum_scatter(weight_part, ('outer', 'inner'), scatter_dimension=0, ti...  1180 us
    select_n x510, other arithmetic, lap(): jnp.where(position < mine, new, old)  422 us
    all_gather x3, waiting for transfers between devices, prefix(): pieces = jax.tree.map(lambda part: lax.all_gather(part, axis), value)  201 us
    psum x1, blocking collectives, per_device(): bias_grads, rate_grad = lax.psum((bias_part, rate_part), ('outer', 'inner'))  75.4 us
    all_gather x3, other arithmetic, prefix(): pieces = jax.tree.map(lambda part: lax.all_gather(part, axis), value)  73.5 us
  transfers between devices with their start and end apart: 4, of which 3 were waited for; matrix products, arithmetic and copies ran while one was open for 15% of the time, Pallas kernels for 0%

commit v1 on v0

v1 whole, which is shorter than its diff:
```python
import functools

import jax
import jax.numpy as jnp
from jax import lax
from jax.experimental import pallas as pl
from jax.experimental.pallas import tpu as pltpu
from jax.sharding import PartitionSpec as P

F32, BF16 = jnp.float32, jnp.bfloat16
rate_gain = 8.0
NY, NZ, NX, NC = 4, 8, 4, 2
GROUP = NX * NC
BLOCKS, BW, D = 16, 256, 4096
SEQS, STEPS = 2, 64
ROWS = SEQS * STEPS
PAIRS = BLOCKS // 2
SLAB = 32
SIZES = {"y": NY, "z": NZ, "x": NX}

HALF = BW // 2

PARTS = (
    ((0, 16, "xyz"), (16, 8, "yxz"), (24, 8, "zxy")),
    ((0, 8, "xyz"), (8, 16, "yxz"), (24, 8, "zxy")),
)


def rounds_of(order):
    rounds = []
    for stage, axis in enumerate(order):
        if stage == 0 or (stage == 1 and order[2] == "z"):
            rounds += [(stage, axis, step) for step in range(1, SIZES[axis] // 2 + 1)]
        else:
            rounds.append((stage, axis, 0))
    return rounds


def free_axes(order, stage):
    return [axis for axis in "yzx" if axis in order[stage + 1 :]]


def lead_shape(axes, halved):
    shape = []
    for position, axis in enumerate(axes):
        half = halved and position == 0
        if axis == "y":
            shape += [1 if half else 2, 2]
        else:
            shape += [SIZES[axis] // 2 if half else SIZES[axis]]
    return tuple(shape)


def landing_buffers():
    places, shapes = {}, []
    for h in range(2):
        for part, (_, rows, order) in enumerate(PARTS[h]):
            for number, (stage, axis, step) in enumerate(rounds_of(order)):
                count = SIZES[axis] if step == 0 else 2
                places[h, part, number] = len(shapes)
                lead = lead_shape(free_axes(order, stage), step == 1)
                shapes.append((count,) + lead + (rows, HALF))
    return places, shapes


LANDING, LANDING_SHAPES = landing_buffers()

EVENTS = [
    (0, 2, 0), (0, 1, 0), (0, 0, 0), (0, 2, 1), "through 0", (0, 1, 1), (1, 2, 0), (0, 2, 2),
    "vector 0", "through 1", (1, 1, 0), (0, 1, 2), (0, 0, 1), (1, 0, 0), (1, 2, 1), (0, 2, 3),
    (0, 1, 3), "vector 1", (0, 0, 2), (1, 2, 2), (0, 2, 4), (1, 0, 1), (0, 1, 4), (1, 1, 1),
    (0, 0, 3), (1, 2, 3), "vector 2", (0, 2, 5), (1, 0, 2), (1, 1, 2), (0, 0, 4), (1, 2, 4),
    (1, 0, 3), (1, 1, 3), "vector 3", (1, 2, 5), (1, 0, 4), (1, 1, 4),
]


def kernel(
    x_hbm, go_hbm, w_hbm, bias_hbm, rate_hbm,
    out_hbm, gg_ref, bg_ref, rg_ref,
    x_v, go_v, w_v, bias_v, rate_v, out_v,
    tri_v, pre_v, ld_v, drive_v, lc_v, split_v, dg_v, p_v,
    inv_v, pex_v, before_v, tail_v, c_v, e_v, f_v, q3_v, q4_v,
    sum_s, sum_r, zsum_r, ysum_r, ent_s, ent_r,
    vec_s, vec_r, vecz_r, vecy_r, veco_r,
    grad_v, part_v,
    in_sem, small_sem, out_sem,
    g1_send, g1_recv, z1_send, z1_recv, y1_send, y1_recv, g2_send, g2_recv,
    v1_send, v1_recv, vz_send, vz_recv, vy_send, vy_recv, v2_send, v2_recv,
    core_send, core_recv, far_send, far_recv,
    *landing,
):
    y = lax.axis_index("outer")
    inner = lax.axis_index("inner")
    z = inner // GROUP
    member = lax.rem(inner, GROUP)
    x = member // NC
    core = lax.rem(member, NC)

    def device(y_at, z_at, member_at):
        return (y_at, z_at * GROUP + member_at)

    barrier = pltpu.get_barrier_semaphore()

    def greet(target):
        pl.semaphore_signal(barrier, inc=1, device_id=target, device_id_type=pl.DeviceIdType.MESH)

    for step in range(1, GROUP):
        greet(device(y, z, lax.rem(member + step, GROUP)))
    for step in range(1, NZ):
        greet(device(y, lax.rem(z + step, NZ), member))
    for step in range(1, NY):
        greet(device(lax.rem(y + step, NY), z, member))

    def start_loads(step, carry):
        blocks = pl.ds(4 * step, 4)
        for b in range(4):
            k = 4 * step + b
            lanes = pl.ds(pl.multiple_of(k * BW, BW), BW)
            pltpu.make_async_copy(x_hbm.at[:, lanes], x_v.at[k], in_sem.at[0, step]).start()
        pltpu.make_async_copy(w_hbm.at[:, blocks], w_v.at[:, blocks], in_sem.at[1, step]).start()
        for b in range(4):
            k = 4 * step + b
            lanes = pl.ds(pl.multiple_of(k * BW, BW), BW)
            pltpu.make_async_copy(go_hbm.at[:, lanes], go_v.at[k], in_sem.at[2, step]).start()
        return carry

    def wait_loads(step):
        blocks = pl.ds(4 * step, 4)
        pltpu.make_async_copy(x_v.at[blocks], x_v.at[blocks], in_sem.at[0, step]).wait()
        pltpu.make_async_copy(w_hbm.at[:, blocks], w_v.at[:, blocks], in_sem.at[1, step]).wait()
        pltpu.make_async_copy(go_v.at[blocks], go_v.at[blocks], in_sem.at[2, step]).wait()

    bias_copy = pltpu.make_async_copy(bias_hbm, bias_v, small_sem.at[0])
    rate_copy = pltpu.make_async_copy(rate_hbm, rate_v, small_sem.at[1])
    bias_copy.start()
    rate_copy.start()
    lax.fori_loop(0, 4, start_loads, 0)

    row = lax.broadcasted_iota(jnp.int32, (ROWS, 2 * ROWS), 0)
    col = lax.broadcasted_iota(jnp.int32, (ROWS, 2 * ROWS), 1)
    col = jnp.where(col >= ROWS, col - ROWS, col)
    same = jnp.where(row >= STEPS, 1, 0) == jnp.where(col >= STEPS, 1, 0)
    tri_v[0] = jnp.where(same & (col <= row), 1.0, 0.0).astype(BF16)
    tri_v[1] = jnp.where(same & (col < row), 1.0, 0.0).astype(BF16)
    tri_v[2] = jnp.where(same & (col >= row), 1.0, 0.0).astype(BF16)

    vec_s[...] = jnp.zeros_like(vec_s)
    sum_s[...] = jnp.zeros_like(sum_s)
    bias_copy.wait()
    rate_copy.wait()

    def slabs():
        for b in range(2):
            for top in range(0, ROWS, SLAB):
                yield b, pl.ds(top, SLAB), pl.ds(b * HALF, HALF)

    def split_store(u, which, top, lanes, value):
        high = value.astype(BF16)
        split_v[u, which, pl.ds(top, SLAB), lanes] = high
        split_v[u, which, pl.ds(ROWS + top, SLAB), lanes] = (value - high.astype(F32)).astype(BF16)

    def gate_columns(k, h):
        lanes = pl.ds(h * HALF, HALF)
        return jnp.concatenate([w_v[0, k, :, lanes], w_v[1, k, :, lanes]], axis=1)

    def local(h, step):
        mine = pl.ds(h * HALF, HALF)
        units = [2 * step, 2 * step + 1]
        if h == 0:
            wait_loads(step)
        for u, m in enumerate(units):
            for b in range(2):
                k = 2 * m + b
                pre_v[u, b] = jnp.dot(x_v[k], gate_columns(k, h), preferred_element_type=F32)
        for u, m in enumerate(units):
            for b, rows, lanes in slabs():
                k = 2 * m + b
                column = pl.ds(pl.multiple_of(k * BW + h * HALF, HALF), HALF)
                rate = rate_v[0:1, column]
                pre_r = pre_v[u, b, rows, pl.ds(0, HALF)] + bias_v[0:1, column]
                pre_i = pre_v[u, b, rows, pl.ds(HALF, HALF)] + bias_v[1:2, column]
                recur = 1.0 / (1.0 + jnp.exp(-pre_r))
                inject = 1.0 / (1.0 + jnp.exp(-pre_i))
                values = x_v[k, rows, mine].astype(F32)
                log_decay = (-rate_gain * rate) * recur
                decay = jnp.exp(log_decay)
                series = -log_decay * (
                    1.0 + log_decay * (0.5 + log_decay * (1.0 / 6.0 + log_decay * (1.0 / 24.0)))
                )
                lost = jnp.where(log_decay > -0.1, series, 1.0 - decay)
                square = lost * (1.0 + decay)
                inverse_scale = lax.rsqrt(square)
                scale = square * inverse_scale
                driven = inject * values
                drive_v[u, rows, lanes] = scale * driven
                ld_v[u, rows, lanes] = log_decay
                split_store(u, 0, rows.start, lanes, log_decay)
                gained = rate_gain * recur
                e = gained * decay
                e_v[h, m, rows, lanes] = e
                c_v[h, m, rows, lanes] = e * decay * driven * inverse_scale
                f_v[h, m, rows, lanes] = rate * (1.0 - recur)
                q4 = scale * inject
                q4_v[h, m, rows, lanes] = q4
                q3_v[h, m, rows, lanes] = q4 * values * (1.0 - inject)
        for u, m in enumerate(units):
            lc_v[u] = jnp.dot(tri_v[0], split_v[u, 0], preferred_element_type=F32)
        for u, m in enumerate(units):
            for b, rows, lanes in slabs():
                log_cum = lc_v[u, rows, lanes]
                cum = jnp.exp(log_cum)
                inverse = jnp.exp(-log_cum)
                inv_v[h, m, rows, lanes] = inverse
                pex_v[h, m, rows, lanes] = jnp.exp(log_cum - ld_v[u, rows, lanes])
                scaled = drive_v[u, rows, lanes] * inverse
                split_store(u, 1, rows.start, lanes, scaled)
                upstream = go_v[2 * m + b, rows, mine].astype(F32)
                split_store(u, 2, rows.start, lanes, cum * upstream)
                last = rows.start + SLAB
                if last % STEPS == 0:
                    slot = (last // STEPS - 1) * 2 + b
                    sum_s[h, m, pl.ds(slot, 1), :] = cum[SLAB - 1 : SLAB]
                    sum_s[h, m, pl.ds(4 + slot, 1), :] = scaled[SLAB - 1 : SLAB]
        for u, m in enumerate(units):
            before_v[h, m] = jnp.dot(tri_v[1], split_v[u, 1], preferred_element_type=F32)
            tail_v[h, m] = jnp.dot(tri_v[2], split_v[u, 2], preferred_element_type=F32)
        for u, m in enumerate(units):
            for s in range(SEQS):
                for b in range(2):
                    slot = s * 2 + b
                    lanes = pl.ds(b * HALF, HALF)
                    before = before_v[h, m, pl.ds(s * STEPS + STEPS - 1, 1), lanes]
                    end = sum_s[h, m, pl.ds(slot, 1), :]
                    held = sum_s[h, m, pl.ds(4 + slot, 1), :]
                    sum_s[h, m, pl.ds(4 + slot, 1), :] = end * (before + held)
                    sum_s[h, m, pl.ds(8 + slot, 1), :] = tail_v[h, m, pl.ds(s * STEPS, 1), lanes]

    def local_steps(h, start, stop):
        def body(step, carry):
            local(h, step)
            return carry

        lax.fori_loop(start, stop, body, 0)

    def remote(src, dst, send, recv, target):
        return pltpu.make_async_remote_copy(
            src_ref=src, dst_ref=dst, send_sem=send, recv_sem=recv,
            device_id=target, device_id_type=pl.DeviceIdType.MESH,
        )

    def in_group(source, landing, send, recv, peer):
        return remote(source.at[peer], landing.at[member], send, recv, device(y, z, peer))

    def along(axis, landing, send, recv, peer):
        here = z if axis == "z" else y
        target = device(y, peer, member) if axis == "z" else device(peer, z, member)
        return remote(landing.at[here], landing.at[here], send, recv, target)

    def all_of(landing, send, recv, count):
        every = landing.at[pl.ds(0, count - 1)]
        return remote(every, every, send, recv, device(y, z, x * NC + (1 - core)))

    def group_all(source, landing, send, recv):
        return all_of(landing, send, recv, GROUP)

    def along_all(axis, landing, send, recv):
        return all_of(landing, send, recv, SIZES[axis])

    def group_peers():
        return [lax.rem(member + step, GROUP) for step in range(1, GROUP)]

    def axis_peers(axis):
        here, size = (z, NZ) if axis == "z" else (y, NY)
        return [lax.rem(here + step, size) for step in range(1, size)]

    mult, first, back = pl.ds(0, 4), pl.ds(4, 4), pl.ds(8, 4)
    ones, zeros = jnp.ones((4, 128), F32), jnp.zeros((4, 128), F32)

    def total_of(ref, count):
        decay = ref[0, mult]
        state = ref[0, first]
        for j in range(1, count):
            state = ref[j, mult] * state + ref[j, first]
            decay = decay * ref[j, mult]
        adjoint = ref[count - 1, back]
        for j in range(count - 2, -1, -1):
            adjoint = ref[j, mult] * adjoint + ref[j, back]
        return decay, state, adjoint

    def put(ref, index, values):
        for position, value in enumerate(values):
            ref[index, pl.ds(4 * position, 4)] = value
        ref[index, pl.ds(12, 4)] = zeros

    def earlier(ref, count, position, decay, state):
        for j in range(count):
            use = j < position
            state = jnp.where(use, ref[j, mult] * state + ref[j, first], state)
            decay = jnp.where(use, ref[j, mult] * decay, decay)
        return decay, state

    def later(ref, count, position, decay, adjoint):
        for j in range(count - 1, -1, -1):
            use = j > position
            adjoint = jnp.where(use, ref[j, mult] * adjoint + ref[j, back], adjoint)
            decay = jnp.where(use, ref[j, mult] * decay, decay)
        return decay, adjoint

    def group_1(h):
        return sum_s.at[h], sum_r.at[h], g1_send.at[h], g1_recv.at[h]

    def group_2(h):
        return ent_s.at[h], ent_r.at[h], g2_send.at[h], g2_recv.at[h]

    def along_z(h):
        return "z", zsum_r.at[h], z1_send.at[h], z1_recv.at[h]

    def along_y(h):
        return "y", ysum_r.at[h], y1_send.at[h], y1_recv.at[h]

    def summaries_out(h):
        for peer in group_peers():
            in_group(*group_1(h), peer).start()
        sum_r[h, member] = sum_s[h, member]

    def to_z(h):
        group_all(*group_1(h)).wait_recv()
        put(zsum_r.at[h], z, total_of(sum_r.at[h], GROUP))
        for peer in axis_peers("z"):
            along(*along_z(h), peer).start()

    def to_y(h):
        along_all(*along_z(h)).wait_recv()
        put(ysum_r.at[h], y, total_of(zsum_r.at[h], NZ))
        for peer in axis_peers("y"):
            along(*along_y(h), peer).start()

    def to_members(h):
        z_decay, z_state = earlier(zsum_r.at[h], NZ, z, ones, zeros)
        z_fade, z_adjoint = later(zsum_r.at[h], NZ, z, ones, zeros)
        along_all(*along_y(h)).wait_recv()
        state = z_decay * earlier(ysum_r.at[h], NY, y, ones, zeros)[1] + z_state
        adjoint = z_fade * later(ysum_r.at[h], NY, y, ones, zeros)[1] + z_adjoint
        for j in range(GROUP):
            ent_s[h, j, pl.ds(0, 4)] = state
            state = sum_r[h, j, mult] * state + sum_r[h, j, first]
        for j in range(GROUP - 1, -1, -1):
            ent_s[h, j, pl.ds(4, 4)] = adjoint
            adjoint = sum_r[h, j, mult] * adjoint + sum_r[h, j, back]
        for peer in group_peers():
            in_group(*group_2(h), peer).start()
        ent_r[h, member] = ent_s[h, member]

    def entered(h):
        group_all(*group_2(h)).wait_recv()

    def summaries_sent():
        for h in range(2):
            group_all(*group_1(h)).wait_send()
            group_all(*group_2(h)).wait_send()
            along_all(*along_z(h)).wait_send()
            along_all(*along_y(h)).wait_send()

    other = device(y, z, x * NC + (1 - core))

    def core_copy(h, m):
        high, low = m // 4, pl.ds(2 * lax.rem(m, 4), 2)
        return remote(
            grad_v.at[h, :, high, low, :, 1 - core], part_v.at[h, :, high, low],
            core_send.at[h], core_recv.at[h], other,
        )

    def core_all(h):
        return remote(part_v.at[h], part_v.at[h], core_send.at[h], core_recv.at[h], other)

    def gradient(h, step):
        units = [2 * step, 2 * step + 1]
        for m in units:
            for b in range(2):
                k = 2 * m + b
                lanes = pl.ds(b * HALF, HALF)
                sums = [jnp.zeros((8, 128), F32) for _ in range(3)]
                for s in range(SEQS):
                    slot = s * 2 + b
                    entering = ent_r[h, m, pl.ds(slot, 1), :]
                    arriving = ent_r[h, m, pl.ds(4 + slot, 1), :] * sum_s[h, m, pl.ds(slot, 1), :]
                    for top in range(s * STEPS, (s + 1) * STEPS, SLAB):
                        rows = pl.ds(top, SLAB)
                        at = (h, m, rows, lanes)
                        adj = inv_v[at] * (tail_v[at] + arriving)
                        previous = pex_v[at] * (before_v[at] + entering)
                        rated = adj * (c_v[at] - previous * e_v[at])
                        pre_r = rated * f_v[at]
                        pre_i = adj * q3_v[at]
                        dg_v[at] = adj * q4_v[at]
                        p_v[k, h, rows, pl.ds(0, HALF)] = pre_r.astype(BF16)
                        p_v[k, h, rows, pl.ds(HALF, HALF)] = pre_i.astype(BF16)
                        for position, value in enumerate((pre_r, pre_i, rated)):
                            for part in range(0, SLAB, 8):
                                sums[position] = sums[position] + value[part : part + 8]
                for position in range(3):
                    line = position * 4 + h * 2 + b
                    vec_s[m, pl.ds(line, 1), :] = jnp.sum(sums[position], axis=0, keepdims=True)
        for m in units:
            for b in range(2):
                k = 2 * m + b
                outer = lax.dot_general(
                    x_v[k], p_v[k, h], (((0,), (0,)), ((), ())), preferred_element_type=F32
                )
                for g in range(2):
                    grad_v[h, g, m // 4, 2 * lax.rem(m, 4) + b] = outer[
                        :, g * HALF : (g + 1) * HALF
                    ].reshape(NX, NC, 32, HALF)
            core_copy(h, m).start()

    def gradient_steps(h, start, stop):
        def body(step, carry):
            gradient(h, step)
            return carry

        lax.fori_loop(start, stop, body, 0)

    def out_copy(k):
        lanes = pl.ds(pl.multiple_of(k * BW, BW), BW)
        return pltpu.make_async_copy(out_v.at[k], out_hbm.at[:, lanes], out_sem)

    def through(half):
        def body(m, carry):
            for b in range(2):
                k = 2 * m + b
                across = (((1,), (1,)), ((), ()))
                for h in range(2):
                    back_in = lax.dot_general(
                        p_v[k, h], gate_columns(k, h), across, preferred_element_type=F32
                    )
                    total = back_in if h == 0 else total + back_in
                for h in range(2):
                    mine = pl.ds(h * HALF, HALF)
                    direct = dg_v[h, m, :, pl.ds(b * HALF, HALF)]
                    out_v[k, :, mine] = (direct + total[:, h * HALF : (h + 1) * HALF]).astype(BF16)
                out_copy(k).start()
            return carry

        lax.fori_loop(half * 4, half * 4 + 4, body, 0)

    def core_sum(h):
        core_all(h).wait_recv()

        def body(m, carry):
            high = m // 4
            for g in range(2):
                for b in range(2):
                    at = 2 * lax.rem(m, 4) + b
                    part_v[h, g, high, at] = part_v[h, g, high, at] + grad_v[h, g, high, at, :, core]
            return carry

        lax.fori_loop(0, PAIRS, body, 0)

    here = {"y": y, "z": z, "x": x}

    def index_of(axis, at, whole, halved, side):
        if not whole:
            return (at // 2, lax.rem(at, 2)) if axis == "y" else (at,)
        if axis == "y":
            return (pl.ds(side, 1) if halved else pl.ds(0, 2), pl.ds(0, 2))
        size = SIZES[axis]
        return (pl.ds(side * (size // 2), size // 2) if halved else pl.ds(0, size),)

    def view(h, part, stage, target, halved, side):
        row0, rows, order = PARTS[h][part]
        axis, axes = order[stage], free_axes(order, stage)
        found = (h,)
        for name in "yzx":
            if name == axis:
                found += index_of(name, target, False, False, 0)
            elif name in axes:
                found += index_of(name, 0, True, halved and name == axes[0], side)
            else:
                found += index_of(name, here[name], False, False, 0)
        return found + (pl.ds(row0, rows), slice(None))

    def far_all(h, part, number):
        buffer = landing[LANDING[h, part, number]]
        axis, step = rounds_of(PARTS[h][part][2])[number][1:]
        every = buffer if step > 0 else buffer.at[pl.ds(0, SIZES[axis] - 1)]
        at = LANDING[h, part, number]
        return remote(every, every, far_send.at[at], far_recv.at[at], other)

    def ring_copy(h, part, number, side):
        stage, axis, step = rounds_of(PARTS[h][part][2])[number]
        size = SIZES[axis]
        half = size // 2
        sent = here[axis] + (half - step + 1 if side == 0 else size - half + step - 1)
        place = dict(here)
        place[axis] = lax.rem(here[axis] + (1 if side == 0 else size - 1), size)
        at = LANDING[h, part, number]
        return remote(
            part_v.at[view(h, part, stage, lax.rem(sent, size), step == 1, side)],
            landing[LANDING[h, part, number]].at[side], far_send.at[at], far_recv.at[at],
            device(place["y"], place["z"], place["x"] * NC + core),
        )

    def direct_copy(h, part, number, peer):
        stage, axis, _ = rounds_of(PARTS[h][part][2])[number]
        place = dict(here)
        place[axis] = peer
        at = LANDING[h, part, number]
        return remote(
            part_v.at[view(h, part, stage, peer, False, 0)],
            landing[LANDING[h, part, number]].at[here[axis]], far_send.at[at], far_recv.at[at],
            device(place["y"], place["z"], place["x"] * NC + core),
        )

    def copies_out(h, part, number):
        _, axis, step = rounds_of(PARTS[h][part][2])[number]
        if step > 0:
            return [ring_copy(h, part, number, side) for side in range(2)]
        peers = [lax.rem(here[axis] + far, SIZES[axis]) for far in range(1, SIZES[axis])]
        return [direct_copy(h, part, number, peer) for peer in peers]

    def far_start(h, part, number):
        for copy in copies_out(h, part, number):
            copy.start()

    def add_landed(at, axes, halved, side, buffer, slots):
        if len(axes) == 0:
            part_v[at] = part_v[at] + sum(buffer[slot] for slot in slots)
            return
        axis = axes[0]
        size = SIZES[axis] // 2 if halved else SIZES[axis]
        position = 1 + {"y": 0, "z": 2, "x": 3}[axis]
        width = 2 if axis == "y" else 1
        base = size * side if halved else 0

        def body(i, carry):
            if axis == "y":
                from_, to = (i // 2, lax.rem(i, 2)), ((base + i) // 2, lax.rem(base + i, 2))
            else:
                from_, to = (i,), (base + i,)
            place = at[:position] + to + at[position + width :]
            part_v[place] = part_v[place] + sum(buffer[(slot,) + from_] for slot in slots)
            return carry

        lax.fori_loop(0, size, body, 0)

    def far_finish(h, part, number):
        order = PARTS[h][part][2]
        stage, axis, step = rounds_of(order)[number]
        size, axes = SIZES[axis], free_axes(order, stage)
        buffer = landing[LANDING[h, part, number]]
        far_all(h, part, number).wait_recv()
        if step == 0:
            peers = [lax.rem(here[axis] + far, size) for far in range(1, size)]
            at = view(h, part, stage, here[axis], False, 0)
            add_landed(at, axes, False, 0, buffer, peers)
            return
        half = size // 2
        for side in range(2):
            came = here[axis] + (half - step if side == 0 else size - half + step)
            at = view(h, part, stage, lax.rem(came, size), step == 1, side)
            add_landed(at, axes, step == 1, side, buffer, [side])

    vector_1 = (vec_s, vec_r, v1_send, v1_recv)
    vector_z = ("z", vecz_r, vz_send, vz_recv)
    vector_y = ("y", vecy_r, vy_send, vy_recv)

    vector_2 = (veco_r, veco_r, v2_send, v2_recv)

    def vector_copy(peer):
        return remote(veco_r.at[member], veco_r.at[member], v2_send, v2_recv, device(y, z, peer))

    def vector_out():
        for peer in group_peers():
            in_group(*vector_1, peer).start()
        vec_r[member] = vec_s[member]

    def vector_step(step):
        if step == 0:
            group_all(*vector_1).wait_recv()
            vecz_r[z] = sum(vec_r[j] for j in range(GROUP))
            for peer in axis_peers("z"):
                along(*vector_z, peer).start()
        elif step == 1:
            along_all(*vector_z).wait_recv()
            vecy_r[y] = sum(vecz_r[j] for j in range(NZ))
            for peer in axis_peers("y"):
                along(*vector_y, peer).start()
        elif step == 2:
            along_all(*vector_y).wait_recv()
            veco_r[member] = sum(vecy_r[j] for j in range(NY))
            for peer in group_peers():
                vector_copy(peer).start()
        else:
            group_all(*vector_2).wait_recv()
            for j in range(GROUP):
                for position in range(3):
                    for h in range(2):
                        for b in range(2):
                            lanes = pl.ds((2 * j + b) * BW + h * HALF, HALF)
                            line = veco_r[j, pl.ds(position * 4 + h * 2 + b, 1), :]
                            if position < 2:
                                bg_ref[pl.ds(position, 1), lanes] = line
                            else:
                                rg_ref[:, lanes] = line

    local_steps(0, 0, 4)
    pl.semaphore_wait(barrier, (GROUP - 1) + (NZ - 1) + (NY - 1))
    summaries_out(0)
    local_steps(1, 0, 3)
    to_z(0)
    local_steps(1, 3, 4)
    summaries_out(1)
    to_y(0)
    to_z(1)
    to_members(0)
    to_y(1)
    entered(0)
    gradient_steps(0, 0, 2)
    to_members(1)
    gradient_steps(0, 2, 4)
    core_sum(0)
    for part in range(3):
        far_start(0, part, 0)
    entered(1)
    gradient_steps(1, 0, 4)
    vector_out()
    core_sum(1)
    for part in range(3):
        far_start(1, part, 0)
    for event in EVENTS:
        if isinstance(event, str):
            kind, number = event.split()
            (through if kind == "through" else vector_step)(int(number))
            continue
        h, part, number = event
        far_finish(h, part, number)
        if number + 1 < len(rounds_of(PARTS[h][part][2])):
            far_start(h, part, number + 1)
    for h in range(2):
        gg_ref[:, pl.ds(h * HALF, HALF)] = part_v[h, y // 2, lax.rem(y, 2), z, x]

    summaries_sent()
    group_all(*vector_1).wait_send()
    group_all(*vector_2).wait_send()
    along_all(*vector_z).wait_send()
    along_all(*vector_y).wait_send()
    for h, part, number in LANDING:
        far_all(h, part, number).wait_send()
    for h in range(2):
        core_all(h).wait_send()
    pltpu.make_async_copy(out_v, out_v, out_sem).wait()


def finish(*refs):
    sources, results, held, sem = refs[:4], refs[4:8], refs[8:12], refs[12]
    count = 0
    pairs = []
    for source, result, hold in zip(sources, results, held):
        rows = source.shape[0]
        size = 16 if rows == ROWS else rows
        for top in range(0, rows, size):
            at = pl.ds(top, size)
            pairs.append((
                pltpu.make_async_copy(source.at[at], hold.at[at], sem.at[0, count]),
                pltpu.make_async_copy(hold.at[at], result.at[at], sem.at[1, count]),
            ))
            count += 1
    for into, _ in pairs:
        into.start()
    for into, out in pairs:
        into.wait()
        out.start()
    for _, out in pairs:
        out.wait()


def per_device(inputs, grad_out, gate_weights, gate_biases, decay_rate):
    shape = inputs.shape
    hbm = pl.BlockSpec(memory_space=pl.ANY)
    vmem = pl.BlockSpec(memory_space=pltpu.VMEM)
    dma = pltpu.SemaphoreType.DMA
    block32 = pltpu.VMEM((2, PAIRS, ROWS, BW), F32)
    block16 = pltpu.VMEM((BLOCKS, ROWS, BW), BF16)
    unit32 = pltpu.VMEM((2, ROWS, BW), F32)
    scratch = [
        block16, block16, pltpu.VMEM((2, BLOCKS, BW, BW), BF16),
        pltpu.VMEM((2, D), F32), pltpu.VMEM((1, D), F32), block16,
        pltpu.VMEM((3, ROWS, 2 * ROWS), BF16), pltpu.VMEM((2, 2, ROWS, BW), F32),
        unit32, unit32, unit32, pltpu.VMEM((2, 3, 2 * ROWS, BW), BF16),
        block32, pltpu.VMEM((BLOCKS, 2, ROWS, BW), BF16),
    ]
    scratch += [block32] * 9
    scratch += [
        pltpu.VMEM((2, GROUP, 16, 128), F32), pltpu.VMEM((2, GROUP, 16, 128), F32),
        pltpu.VMEM((2, NZ, 16, 128), F32), pltpu.VMEM((2, NY, 16, 128), F32),
        pltpu.VMEM((2, GROUP, 8, 128), F32), pltpu.VMEM((2, GROUP, 8, 128), F32),
        pltpu.VMEM((GROUP, 16, 128), F32), pltpu.VMEM((GROUP, 16, 128), F32),
        pltpu.VMEM((NZ, 16, 128), F32), pltpu.VMEM((NY, 16, 128), F32),
        pltpu.VMEM((GROUP, 16, 128), F32),
        pltpu.VMEM((2, 2, 2, NZ, NX, NC, 32, HALF), F32),
        pltpu.VMEM((2, 2, 2, NZ, NX, 32, HALF), F32),
        dma((3, 4)), dma((2,)), dma(()),
        dma((2,)), dma((2,)), dma((2,)), dma((2,)), dma((2,)), dma((2,)), dma((2,)), dma((2,)),
        dma(()), dma(()), dma(()), dma(()), dma(()), dma(()), dma(()), dma(()),
        dma((2,)), dma((2,)), dma((len(LANDING),)), dma((len(LANDING),)),
    ]
    scratch += [pltpu.VMEM(found, F32) for found in LANDING_SHAPES]
    shapes = (
        jax.ShapeDtypeStruct((ROWS, D), BF16),
        jax.ShapeDtypeStruct((32, BW), F32),
        jax.ShapeDtypeStruct((2, D), F32),
        jax.ShapeDtypeStruct((1, D), F32),
    )
    results = pl.pallas_call(
        kernel,
        out_shape=shapes,
        in_specs=[hbm] * 5,
        out_specs=(hbm, vmem, vmem, vmem),
        scratch_shapes=scratch,
        compiler_params=pltpu.CompilerParams(
            collective_id=0, has_side_effects=True, vmem_limit_bytes=60 * 2**20
        ),
    )(
        inputs.reshape(ROWS, D), grad_out.reshape(ROWS, D), gate_weights,
        gate_biases, decay_rate.reshape(1, D),
    )
    input_grad, gate_grads, bias_grads, rate_grad = pl.pallas_call(
        finish, out_shape=shapes, in_specs=[hbm] * 4, out_specs=[hbm] * 4,
        scratch_shapes=[pltpu.VMEM(found.shape, found.dtype) for found in shapes] + [dma((2, 11))],
    )(*results)
    return (input_grad.reshape(shape), gate_grads, bias_grads, rate_grad.reshape(D))


def solution(mesh):
    in_specs = (P(None, ("outer", "inner"), None), P(None, ("outer", "inner"), None), P(), P(), P())
    out_specs = (P(None, ("outer", "inner"), None), P(("outer", "inner"), None), P(), P())
    return jax.shard_map(
        per_device, mesh=mesh, in_specs=in_specs, out_specs=out_specs, check_vma=False
    )
```

time: 2130 us -> 75.2 us (0.04)
  the two profiles are of different devices: /device:TPU:1 before, /device:TPU:8 now
where the time goes in v1:
time: 75.2 us; the launch traced here: 75.1 us
  Pallas kernels  74.5 us (99%)
    pallas_call x1, Pallas kernels, per_device(): pl.pallas_call(kernel, out_shape=shapes, in_specs=[hbm] * 5, out_specs=(h...  72.3 us
    pallas_call x1, Pallas kernels, per_device(): pl.pallas_call(finish, out_shape=shapes, in_specs=[hbm] * 4, out_specs=[h...  2.16 us

profile of v1, /device:TPU:8, one launch (start us, length us, event | category | flops | bytes accessed | tf_op | source)
XLA Modules:
  0.0 75.1 jit_solution(640946782952406652)
XLA Ops:
  0.6 72.3 %shard_map.84 = (bf16[128,4096]{1,0:T(8,128)(2,1)}, f32[32,256]{1,0:T(8,128)}, f32[2,4096]{1,0:T(2,128)}, f32[1,4096]{1,0:T(1,128)}) custom-call(bf16[128,4096]{1,0:T(8,128)(2,1)} %bitcast.5, bf16[128,4096]{1,0:T(8,128)(2,1)} %bitcast.6, bf16[2,16,256,256]{3,2,1,0:T(8,128)(2,1)} %w_hbm.1, f32[2,4096]{1,0:T(2,128)} %bias_hbm.1, f32[1,4096]{1,0:T(1,128)} %bitcast.7), custom_call_target="tpu_custom_call" | custom-call | tf_op jit(solution)/shard_map/pallas_call | solution.py:714
  72.9 2.2 %shard_map.85 = (bf16[128,4096]{1,0:T(8,128)(2,1)}, f32[32,256]{1,0:T(8,128)}, f32[2,4096]{1,0:T(2,128)}, f32[1,4096]{1,0:T(1,128)}) custom-call(bf16[128,4096]{1,0:T(8,128)(2,1)} %get-tuple-element.12.refs_0_, f32[32,256]{1,0:T(8,128)} %get-tuple-element.13.refs_1_, f32[2,4096]{1,0:T(2,128)} %get-tuple-element.14.refs_2_, f32[1,4096]{1,0:T(1,128)} %get-tuple-element.15.refs_3_), custom_call_target="tpu_custom_call" | custom-call | tf_op jit(solution)/shard_map/pallas_call | solution.py:727

commit v2 on v1

--- a/solution.py
+++ b/solution.py
@@ -21,15 +21,15 @@
 HALF = BW // 2
 
 PARTS = (
-    ((0, 16, "xyz"), (16, 8, "yxz"), (24, 8, "zxy")),
-    ((0, 8, "xyz"), (8, 16, "yxz"), (24, 8, "zxy")),
+    ((0, 8, "zyx"), (8, 16, "zxy"), (24, 8, "xyz")),
+    ((0, 16, "yxz"), (16, 8, "xyz"), (24, 8, "xyz")),
 )
 
 
 def rounds_of(order):
     rounds = []
     for stage, axis in enumerate(order):
-        if stage == 0 or (stage == 1 and order[2] == "z"):
+        if stage == 0:
             rounds += [(stage, axis, step) for step in range(1, SIZES[axis] // 2 + 1)]
         else:
             rounds.append((stage, axis, 0))
@@ -66,11 +66,11 @@
 LANDING, LANDING_SHAPES = landing_buffers()
 
 EVENTS = [
-    (0, 2, 0), (0, 1, 0), (0, 0, 0), (0, 2, 1), "through 0", (0, 1, 1), (1, 2, 0), (0, 2, 2),
-    "vector 0", "through 1", (1, 1, 0), (0, 1, 2), (0, 0, 1), (1, 0, 0), (1, 2, 1), (0, 2, 3),
-    (0, 1, 3), "vector 1", (0, 0, 2), (1, 2, 2), (0, 2, 4), (1, 0, 1), (0, 1, 4), (1, 1, 1),
-    (0, 0, 3), (1, 2, 3), "vector 2", (0, 2, 5), (1, 0, 2), (1, 1, 2), (0, 0, 4), (1, 2, 4),
-    (1, 0, 3), (1, 1, 3), "vector 3", (1, 2, 5), (1, 0, 4), (1, 1, 4),
+    (0, 0, 0), (0, 2, 0), (0, 1, 0), (0, 0, 1), "through 0", (0, 2, 1), (0, 1, 1), "through 1",
+    (1, 1, 0), (0, 0, 2), "vector 0", (1, 0, 0), (1, 2, 0), "through 2", (0, 2, 2), (0, 1, 2),
+    (0, 0, 3), (1, 1, 1), "vector 1", "through 3", (1, 2, 1), (0, 2, 3), (1, 0, 1), (0, 1, 3),
+    "vector 2", (0, 0, 4), (1, 1, 2), (1, 2, 2), (1, 0, 2), "vector 3", (0, 1, 4), (0, 0, 5),
+    (1, 1, 3), (1, 2, 3), (0, 1, 5), (1, 0, 3),
 ]
 
 
@@ -111,7 +111,11 @@
     for step in range(1, NY):
         greet(device(lax.rem(y + step, NY), z, member))
 
-    def start_loads(step, carry):
+    def chip_at(turn):
+        return lax.rem(x + 1 + turn, NX)
+
+    def start_loads(turn, carry):
+        step = chip_at(turn)
         blocks = pl.ds(4 * step, 4)
         for b in range(4):
             k = 4 * step + b
@@ -195,14 +199,9 @@
                 drive_v[u, rows, lanes] = scale * driven
                 ld_v[u, rows, lanes] = log_decay
                 split_store(u, 0, rows.start, lanes, log_decay)
-                gained = rate_gain * recur
-                e = gained * decay
-                e_v[h, m, rows, lanes] = e
-                c_v[h, m, rows, lanes] = e * decay * driven * inverse_scale
-                f_v[h, m, rows, lanes] = rate * (1.0 - recur)
-                q4 = scale * inject
-                q4_v[h, m, rows, lanes] = q4
-                q3_v[h, m, rows, lanes] = q4 * values * (1.0 - inject)
+                at = (h, m, rows, lanes)
+                e_v[at], c_v[at], f_v[at] = decay, inverse_scale, recur
+                q4_v[at], q3_v[at] = scale, inject
         for u, m in enumerate(units):
             lc_v[u] = jnp.dot(tri_v[0], split_v[u, 0], preferred_element_type=F32)
         for u, m in enumerate(units):
@@ -235,12 +234,24 @@
                     sum_s[h, m, pl.ds(4 + slot, 1), :] = end * (before + held)
                     sum_s[h, m, pl.ds(8 + slot, 1), :] = tail_v[h, m, pl.ds(s * STEPS, 1), lanes]
 
-    def local_steps(h, start, stop):
-        def body(step, carry):
-            local(h, step)
+    def factors(h):
+        def body(m, carry):
+            for b, rows, lanes in slabs():
+                k = 2 * m + b
+                at = (h, m, rows, lanes)
+                rate = rate_v[0:1, pl.ds(pl.multiple_of(k * BW + h * HALF, HALF), HALF)]
+                values = x_v[k, rows, pl.ds(h * HALF, HALF)].astype(F32)
+                recur, inject, decay = f_v[at], q3_v[at], e_v[at]
+                e = (rate_gain * recur) * decay
+                e_v[at] = e
+                c_v[at] = e * decay * (inject * values) * c_v[at]
+                f_v[at] = rate * (1.0 - recur)
+                q4 = q4_v[at] * inject
+                q4_v[at] = q4
+                q3_v[at] = q4 * values * (1.0 - inject)
             return carry
 
-        lax.fori_loop(start, stop, body, 0)
+        lax.fori_loop(0, PAIRS, body, 0)
 
     def remote(src, dst, send, recv, target):
         return pltpu.make_async_remote_copy(
@@ -266,12 +277,15 @@
     def along_all(axis, landing, send, recv):
         return all_of(landing, send, recv, SIZES[axis])
 
+    def far_first(size):
+        return sorted(range(1, size), key=lambda step: -min(step, size - step))
+
     def group_peers():
-        return [lax.rem(member + step, GROUP) for step in range(1, GROUP)]
+        return [lax.rem(member + step, GROUP) for step in far_first(GROUP)]
 
     def axis_peers(axis):
         here, size = (z, NZ) if axis == "z" else (y, NY)
-        return [lax.rem(here + step, size) for step in range(1, size)]
+        return [lax.rem(here + step, size) for step in far_first(size)]
 
     mult, first, back = pl.ds(0, 4), pl.ds(4, 4), pl.ds(8, 4)
     ones, zeros = jnp.ones((4, 128), F32), jnp.zeros((4, 128), F32)
@@ -318,9 +332,19 @@
     def along_y(h):
         return "y", ysum_r.at[h], y1_send.at[h], y1_recv.at[h]
 
-    def summaries_out(h):
-        for peer in group_peers():
-            in_group(*group_1(h), peer).start()
+    def local_turns(h, stop):
+        def body(turn, carry):
+            chip = chip_at(turn)
+            local(h, chip)
+            for c in range(NC):
+                in_group(*group_1(h), chip * NC + c).start()
+            return carry
+
+        lax.fori_loop(0, stop, body, 0)
+
+    def last_turn(h):
+        local(h, x)
+        in_group(*group_1(h), x * NC + (1 - core)).start()
         sum_r[h, member] = sum_s[h, member]
 
     def to_z(h):
@@ -424,7 +448,7 @@
         lanes = pl.ds(pl.multiple_of(k * BW, BW), BW)
         return pltpu.make_async_copy(out_v.at[k], out_hbm.at[:, lanes], out_sem)
 
-    def through(half):
+    def through(quarter):
         def body(m, carry):
             for b in range(2):
                 k = 2 * m + b
@@ -441,7 +465,7 @@
                 out_copy(k).start()
             return carry
 
-        lax.fori_loop(half * 4, half * 4 + 4, body, 0)
+        lax.fori_loop(2 * quarter, 2 * quarter + 2, body, 0)
 
     def core_sum(h):
         core_all(h).wait_recv()
@@ -515,7 +539,7 @@
         _, axis, step = rounds_of(PARTS[h][part][2])[number]
         if step > 0:
             return [ring_copy(h, part, number, side) for side in range(2)]
-        peers = [lax.rem(here[axis] + far, SIZES[axis]) for far in range(1, SIZES[axis])]
+        peers = [lax.rem(here[axis] + far, SIZES[axis]) for far in far_first(SIZES[axis])]
         return [direct_copy(h, part, number, peer) for peer in peers]
 
     def far_start(h, part, number):
@@ -603,15 +627,16 @@
                             else:
                                 rg_ref[:, lanes] = line
 
-    local_steps(0, 0, 4)
     pl.semaphore_wait(barrier, (GROUP - 1) + (NZ - 1) + (NY - 1))
-    summaries_out(0)
-    local_steps(1, 0, 3)
+    local_turns(0, NX - 1)
+    last_turn(0)
+    local_turns(1, NX - 1)
     to_z(0)
-    local_steps(1, 3, 4)
-    summaries_out(1)
+    last_turn(1)
+    factors(0)
     to_y(0)
     to_z(1)
+    factors(1)
     to_members(0)
     to_y(1)
     entered(0)

time: 75.2 us -> 71.8 us (0.955)
  the two profiles are of different devices: /device:TPU:8 before, /device:TPU:1 now
where the time goes in v2:
time: 71.8 us; the launch traced here: 71.7 us
  Pallas kernels  71.1 us (99%)
    pallas_call x1, Pallas kernels, per_device(): pl.pallas_call(kernel, out_shape=shapes, in_specs=[hbm] * 5, out_specs=(h...  68.9 us
    pallas_call x1, Pallas kernels, per_device(): pl.pallas_call(finish, out_shape=shapes, in_specs=[hbm] * 4, out_specs=[h...  2.16 us

profile of v2, /device:TPU:1, one launch (start us, length us, event | category | flops | bytes accessed | tf_op | source)
XLA Modules:
  0.0 71.7 jit_solution(8318058442818714208)
XLA Ops:
  0.6 68.9 %shard_map.84 = (bf16[128,4096]{1,0:T(8,128)(2,1)}, f32[32,256]{1,0:T(8,128)}, f32[2,4096]{1,0:T(2,128)}, f32[1,4096]{1,0:T(1,128)}) custom-call(bf16[128,4096]{1,0:T(8,128)(2,1)} %bitcast.5, bf16[128,4096]{1,0:T(8,128)(2,1)} %bitcast.6, bf16[2,16,256,256]{3,2,1,0:T(8,128)(2,1)} %w_hbm.1, f32[2,4096]{1,0:T(2,128)} %bias_hbm.1, f32[1,4096]{1,0:T(1,128)} %bitcast.7), custom_call_target="tpu_custom_call" | custom-call | tf_op jit(solution)/shard_map/pallas_call | solution.py:739
  69.6 2.2 %shard_map.85 = (bf16[128,4096]{1,0:T(8,128)(2,1)}, f32[32,256]{1,0:T(8,128)}, f32[2,4096]{1,0:T(2,128)}, f32[1,4096]{1,0:T(1,128)}) custom-call(bf16[128,4096]{1,0:T(8,128)(2,1)} %get-tuple-element.12.refs_0_, f32[32,256]{1,0:T(8,128)} %get-tuple-element.13.refs_1_, f32[2,4096]{1,0:T(2,128)} %get-tuple-element.14.refs_2_, f32[1,4096]{1,0:T(1,128)} %get-tuple-element.15.refs_3_), custom_call_target="tpu_custom_call" | custom-call | tf_op jit(solution)/shard_map/pallas_call | solution.py:752

commit v3 on v2

--- a/solution.py
+++ b/solution.py
@@ -21,8 +21,8 @@
 HALF = BW // 2
 
 PARTS = (
-    ((0, 8, "zyx"), (8, 16, "zxy"), (24, 8, "xyz")),
-    ((0, 16, "yxz"), (16, 8, "xyz"), (24, 8, "xyz")),
+    ((0, 16, "zyx"), (16, 8, "zxy"), (24, 8, "yxz")),
+    ((0, 16, "xyz"), (16, 8, "yxz"), (24, 8, "yxz")),
 )
 
 
@@ -66,11 +66,11 @@
 LANDING, LANDING_SHAPES = landing_buffers()
 
 EVENTS = [
-    (0, 0, 0), (0, 2, 0), (0, 1, 0), (0, 0, 1), "through 0", (0, 2, 1), (0, 1, 1), "through 1",
-    (1, 1, 0), (0, 0, 2), "vector 0", (1, 0, 0), (1, 2, 0), "through 2", (0, 2, 2), (0, 1, 2),
-    (0, 0, 3), (1, 1, 1), "vector 1", "through 3", (1, 2, 1), (0, 2, 3), (1, 0, 1), (0, 1, 3),
-    "vector 2", (0, 0, 4), (1, 1, 2), (1, 2, 2), (1, 0, 2), "vector 3", (0, 1, 4), (0, 0, 5),
-    (1, 1, 3), (1, 2, 3), (0, 1, 5), (1, 0, 3),
+    (0, 0, 0), (0, 2, 0), (0, 1, 0), "through 0", "through 1", "through 2", (0, 0, 1), (0, 2, 1),
+    "vector 0", (0, 1, 1), (1, 0, 0), (1, 1, 0), (1, 2, 0), "through 3", (0, 2, 2), (0, 0, 2),
+    "vector 1", (0, 1, 2), (1, 1, 1), (1, 0, 1), (1, 2, 1), "vector 2", (0, 2, 3), (0, 0, 3),
+    (1, 1, 2), (0, 1, 3), "vector 3", (1, 2, 2), (1, 0, 2), (0, 0, 4), (0, 1, 4), (1, 1, 3),
+    (1, 2, 3), (0, 0, 5), (0, 1, 5), (1, 0, 3),
 ]
 
 
@@ -78,8 +78,8 @@
     x_hbm, go_hbm, w_hbm, bias_hbm, rate_hbm,
     out_hbm, gg_ref, bg_ref, rg_ref,
     x_v, go_v, w_v, bias_v, rate_v, out_v,
-    tri_v, pre_v, ld_v, drive_v, lc_v, split_v, dg_v, p_v,
-    inv_v, pex_v, before_v, tail_v, c_v, e_v, f_v, q3_v, q4_v,
+    tri_v, pre_v, drive_v, lc_v, split_v, dg_v, p_v,
+    inv_v, cum_v, before_v, tail_v, c_v, e_v, f_v, q3_v, q4_v,
     sum_s, sum_r, zsum_r, ysum_r, ent_s, ent_r,
     vec_s, vec_r, vecz_r, vecy_r, veco_r,
     grad_v, part_v,
@@ -197,7 +197,6 @@
                 scale = square * inverse_scale
                 driven = inject * values
                 drive_v[u, rows, lanes] = scale * driven
-                ld_v[u, rows, lanes] = log_decay
                 split_store(u, 0, rows.start, lanes, log_decay)
                 at = (h, m, rows, lanes)
                 e_v[at], c_v[at], f_v[at] = decay, inverse_scale, recur
@@ -210,7 +209,7 @@
                 cum = jnp.exp(log_cum)
                 inverse = jnp.exp(-log_cum)
                 inv_v[h, m, rows, lanes] = inverse
-                pex_v[h, m, rows, lanes] = jnp.exp(log_cum - ld_v[u, rows, lanes])
+                cum_v[h, m, rows, lanes] = cum
                 scaled = drive_v[u, rows, lanes] * inverse
                 split_store(u, 1, rows.start, lanes, scaled)
                 upstream = go_v[2 * m + b, rows, mine].astype(F32)
@@ -242,9 +241,9 @@
                 rate = rate_v[0:1, pl.ds(pl.multiple_of(k * BW + h * HALF, HALF), HALF)]
                 values = x_v[k, rows, pl.ds(h * HALF, HALF)].astype(F32)
                 recur, inject, decay = f_v[at], q3_v[at], e_v[at]
-                e = (rate_gain * recur) * decay
+                e = rate_gain * recur
                 e_v[at] = e
-                c_v[at] = e * decay * (inject * values) * c_v[at]
+                c_v[at] = e * (decay * decay) * (inject * values) * c_v[at]
                 f_v[at] = rate * (1.0 - recur)
                 q4 = q4_v[at] * inject
                 q4_v[at] = q4
@@ -332,7 +331,7 @@
     def along_y(h):
         return "y", ysum_r.at[h], y1_send.at[h], y1_recv.at[h]
 
-    def local_turns(h, stop):
+    def local_turns(h, start, stop):
         def body(turn, carry):
             chip = chip_at(turn)
             local(h, chip)
@@ -340,7 +339,7 @@
                 in_group(*group_1(h), chip * NC + c).start()
             return carry
 
-        lax.fori_loop(0, stop, body, 0)
+        lax.fori_loop(start, stop, body, 0)
 
     def last_turn(h):
         local(h, x)
@@ -391,11 +390,12 @@
         high, low = m // 4, pl.ds(2 * lax.rem(m, 4), 2)
         return remote(
             grad_v.at[h, :, high, low, :, 1 - core], part_v.at[h, :, high, low],
-            core_send.at[h], core_recv.at[h], other,
+            core_send.at[h, high], core_recv.at[h, high], other,
         )
 
-    def core_all(h):
-        return remote(part_v.at[h], part_v.at[h], core_send.at[h], core_recv.at[h], other)
+    def core_all(h, high):
+        every = part_v.at[h, :, high]
+        return remote(every, every, core_send.at[h, high], core_recv.at[h, high], other)
 
     def gradient(h, step):
         units = [2 * step, 2 * step + 1]
@@ -412,8 +412,8 @@
                         rows = pl.ds(top, SLAB)
                         at = (h, m, rows, lanes)
                         adj = inv_v[at] * (tail_v[at] + arriving)
-                        previous = pex_v[at] * (before_v[at] + entering)
-                        rated = adj * (c_v[at] - previous * e_v[at])
+                        carried = cum_v[at] * (before_v[at] + entering)
+                        rated = adj * (c_v[at] - carried * e_v[at])
                         pre_r = rated * f_v[at]
                         pre_i = adj * q3_v[at]
                         dg_v[at] = adj * q4_v[at]
@@ -437,12 +437,12 @@
                     ].reshape(NX, NC, 32, HALF)
             core_copy(h, m).start()
 
-    def gradient_steps(h, start, stop):
+    def gradients(h, high):
         def body(step, carry):
-            gradient(h, step)
+            gradient(h, 2 * high + step)
             return carry
 
-        lax.fori_loop(start, stop, body, 0)
+        lax.fori_loop(0, 2, body, 0)
 
     def out_copy(k):
         lanes = pl.ds(pl.multiple_of(k * BW, BW), BW)
@@ -467,18 +467,15 @@
 
         lax.fori_loop(2 * quarter, 2 * quarter + 2, body, 0)
 
-    def core_sum(h):
-        core_all(h).wait_recv()
-
-        def body(m, carry):
-            high = m // 4
+    def core_sum(h, high):
+        core_all(h, high).wait_recv()
+
+        def body(at, carry):
             for g in range(2):
-                for b in range(2):
-                    at = 2 * lax.rem(m, 4) + b
-                    part_v[h, g, high, at] = part_v[h, g, high, at] + grad_v[h, g, high, at, :, core]
+                part_v[h, g, high, at] = part_v[h, g, high, at] + grad_v[h, g, high, at, :, core]
             return carry
 
-        lax.fori_loop(0, PAIRS, body, 0)
+        lax.fori_loop(0, NZ, body, 0)
 
     here = {"y": y, "z": z, "x": x}
 
@@ -628,30 +625,39 @@
                                 rg_ref[:, lanes] = line
 
     pl.semaphore_wait(barrier, (GROUP - 1) + (NZ - 1) + (NY - 1))
-    local_turns(0, NX - 1)
+    local_turns(0, 0, NX - 1)
     last_turn(0)
-    local_turns(1, NX - 1)
+    local_turns(1, 0, 1)
     to_z(0)
+    local_turns(1, 1, NX - 1)
     last_turn(1)
     factors(0)
-    to_y(0)
     to_z(1)
     factors(1)
+    to_y(0)
     to_members(0)
     to_y(1)
     entered(0)
-    gradient_steps(0, 0, 2)
     to_members(1)
-    gradient_steps(0, 2, 4)
-    core_sum(0)
-    for part in range(3):
+    for high in range(2):
+        gradients(0, high)
+    for high in range(2):
+        core_sum(0, high)
+    for part in range(len(PARTS[0])):
         far_start(0, part, 0)
     entered(1)
-    gradient_steps(1, 0, 4)
+    soon = lax.rem(y, 2)
+    gradients(1, soon)
+    gradients(1, 1 - soon)
+    core_sum(1, soon)
+    for part, (_, _, order) in enumerate(PARTS[1]):
+        if order[0] == "y":
+            far_start(1, part, 0)
     vector_out()
-    core_sum(1)
-    for part in range(3):
-        far_start(1, part, 0)
+    core_sum(1, 1 - soon)
+    for part, (_, _, order) in enumerate(PARTS[1]):
+        if order[0] != "y":
+            far_start(1, part, 0)
     for event in EVENTS:
         if isinstance(event, str):
             kind, number = event.split()
@@ -672,7 +678,8 @@
     for h, part, number in LANDING:
         far_all(h, part, number).wait_send()
     for h in range(2):
-        core_all(h).wait_send()
+        for high in range(2):
+            core_all(h, high).wait_send()
     pltpu.make_async_copy(out_v, out_v, out_sem).wait()
 
 
@@ -711,7 +718,7 @@
         block16, block16, pltpu.VMEM((2, BLOCKS, BW, BW), BF16),
         pltpu.VMEM((2, D), F32), pltpu.VMEM((1, D), F32), block16,
         pltpu.VMEM((3, ROWS, 2 * ROWS), BF16), pltpu.VMEM((2, 2, ROWS, BW), F32),
-        unit32, unit32, unit32, pltpu.VMEM((2, 3, 2 * ROWS, BW), BF16),
+        unit32, unit32, pltpu.VMEM((2, 3, 2 * ROWS, BW), BF16),
         block32, pltpu.VMEM((BLOCKS, 2, ROWS, BW), BF16),
     ]
     scratch += [block32] * 9
@@ -727,7 +734,7 @@
         dma((3, 4)), dma((2,)), dma(()),
         dma((2,)), dma((2,)), dma((2,)), dma((2,)), dma((2,)), dma((2,)), dma((2,)), dma((2,)),
         dma(()), dma(()), dma(()), dma(()), dma(()), dma(()), dma(()), dma(()),
-        dma((2,)), dma((2,)), dma((len(LANDING),)), dma((len(LANDING),)),
+        dma((2, 2)), dma((2, 2)), dma((len(LANDING),)), dma((len(LANDING),)),
     ]
     scratch += [pltpu.VMEM(found, F32) for found in LANDING_SHAPES]
     shapes = (

time: 71.8 us -> 67.8 us (0.944)
  Pallas kernels: 71.1 us -> 66.9 us
    pallas_call x1, Pallas kernels: 68.9 us -> 64.8 us  [per_device(): pl.pallas_call(kernel, out_shape=shapes, in_specs=[hbm] * 5, out_specs=(h...]
where the time goes in v3:
time: 67.8 us; the launch traced here: 67.6 us
  Pallas kernels  66.9 us (99%)
    pallas_call x1, Pallas kernels, per_device(): pl.pallas_call(kernel, out_shape=shapes, in_specs=[hbm] * 5, out_specs=(h...  64.8 us
    pallas_call x1, Pallas kernels, per_device(): pl.pallas_call(finish, out_shape=shapes, in_specs=[hbm] * 4, out_specs=[h...  2.16 us

profile of v3, /device:TPU:1, one launch (start us, length us, event | category | flops | bytes accessed | tf_op | source)
XLA Modules:
  0.0 67.6 jit_solution(11454796962011380378)
XLA Ops:
  0.6 64.8 %shard_map.84 = (bf16[128,4096]{1,0:T(8,128)(2,1)}, f32[32,256]{1,0:T(8,128)}, f32[2,4096]{1,0:T(2,128)}, f32[1,4096]{1,0:T(1,128)}) custom-call(bf16[128,4096]{1,0:T(8,128)(2,1)} %bitcast.5, bf16[128,4096]{1,0:T(8,128)(2,1)} %bitcast.6, bf16[2,16,256,256]{3,2,1,0:T(8,128)(2,1)} %w_hbm.1, f32[2,4096]{1,0:T(2,128)} %bias_hbm.1, f32[1,4096]{1,0:T(1,128)} %bitcast.7), custom_call_target="tpu_custom_call" | custom-call | tf_op jit(solution)/shard_map/pallas_call | solution.py:746
  65.4 2.2 %shard_map.85 = (bf16[128,4096]{1,0:T(8,128)(2,1)}, f32[32,256]{1,0:T(8,128)}, f32[2,4096]{1,0:T(2,128)}, f32[1,4096]{1,0:T(1,128)}) custom-call(bf16[128,4096]{1,0:T(8,128)(2,1)} %get-tuple-element.12.refs_0_, f32[32,256]{1,0:T(8,128)} %get-tuple-element.13.refs_1_, f32[2,4096]{1,0:T(2,128)} %get-tuple-element.14.refs_2_, f32[1,4096]{1,0:T(1,128)} %get-tuple-element.15.refs_3_), custom_call_target="tpu_custom_call" | custom-call | tf_op jit(solution)/shard_map/pallas_call | solution.py:759

commit v4 on v3

--- a/solution.py
+++ b/solution.py
@@ -386,16 +386,19 @@
 
     other = device(y, z, x * NC + (1 - core))
 
+    def batch_of(h, m):
+        return lax.rem(m, 4) // 2 if h == 0 else m // 4
+
     def core_copy(h, m):
         high, low = m // 4, pl.ds(2 * lax.rem(m, 4), 2)
         return remote(
             grad_v.at[h, :, high, low, :, 1 - core], part_v.at[h, :, high, low],
-            core_send.at[h, high], core_recv.at[h, high], other,
+            core_send.at[h, batch_of(h, m)], core_recv.at[h, batch_of(h, m)], other,
         )
 
-    def core_all(h, high):
-        every = part_v.at[h, :, high]
-        return remote(every, every, core_send.at[h, high], core_recv.at[h, high], other)
+    def core_all(h, batch):
+        every = part_v.at[h, :, :, pl.ds(4 * batch, 4)] if h == 0 else part_v.at[h, :, batch]
+        return remote(every, every, core_send.at[h, batch], core_recv.at[h, batch], other)
 
     def gradient(h, step):
         units = [2 * step, 2 * step + 1]
@@ -437,9 +440,9 @@
                     ].reshape(NX, NC, 32, HALF)
             core_copy(h, m).start()
 
-    def gradients(h, high):
+    def gradients(h, batch):
         def body(step, carry):
-            gradient(h, 2 * high + step)
+            gradient(h, batch + 2 * step if h == 0 else 2 * batch + step)
             return carry
 
         lax.fori_loop(0, 2, body, 0)
@@ -467,15 +470,16 @@
 
         lax.fori_loop(2 * quarter, 2 * quarter + 2, body, 0)
 
-    def core_sum(h, high):
-        core_all(h, high).wait_recv()
-
-        def body(at, carry):
+    def core_sum(h, batch):
+        core_all(h, batch).wait_recv()
+
+        def body(i, carry):
+            high, at = (i // 4, 4 * batch + lax.rem(i, 4)) if h == 0 else (batch, i)
             for g in range(2):
                 part_v[h, g, high, at] = part_v[h, g, high, at] + grad_v[h, g, high, at, :, core]
             return carry
 
-        lax.fori_loop(0, NZ, body, 0)
+        lax.fori_loop(0, 8, body, 0)
 
     here = {"y": y, "z": z, "x": x}
 
@@ -639,12 +643,17 @@
     to_y(1)
     entered(0)
     to_members(1)
-    for high in range(2):
-        gradients(0, high)
-    for high in range(2):
-        core_sum(0, high)
-    for part in range(len(PARTS[0])):
-        far_start(0, part, 0)
+    far_z = 1 - z // 4
+    gradients(0, far_z)
+    gradients(0, 1 - far_z)
+    core_sum(0, far_z)
+    for part, (_, _, order) in enumerate(PARTS[0]):
+        if order[0] == "z":
+            far_start(0, part, 0)
+    core_sum(0, 1 - far_z)
+    for part, (_, _, order) in enumerate(PARTS[0]):
+        if order[0] != "z":
+            far_start(0, part, 0)
     entered(1)
     soon = lax.rem(y, 2)
     gradients(1, soon)

time: 67.8 us -> 67.7 us (level)
  no operation moved by 1% of the time
where the time goes in v4:
time: 67.7 us; the launch traced here: 67.6 us
  Pallas kernels  66.9 us (99%)
    pallas_call x1, Pallas kernels, per_device(): pl.pallas_call(kernel, out_shape=shapes, in_specs=[hbm] * 5, out_specs=(h...  64.8 us
    pallas_call x1, Pallas kernels, per_device(): pl.pallas_call(finish, out_shape=shapes, in_specs=[hbm] * 4, out_specs=[h...  2.16 us

profile of v4, /device:TPU:1, one launch (start us, length us, event | category | flops | bytes accessed | tf_op | source)
XLA Modules:
  0.0 67.6 jit_solution(9412837286892784665)
XLA Ops:
  0.6 64.8 %shard_map.84 = (bf16[128,4096]{1,0:T(8,128)(2,1)}, f32[32,256]{1,0:T(8,128)}, f32[2,4096]{1,0:T(2,128)}, f32[1,4096]{1,0:T(1,128)}) custom-call(bf16[128,4096]{1,0:T(8,128)(2,1)} %bitcast.5, bf16[128,4096]{1,0:T(8,128)(2,1)} %bitcast.6, bf16[2,16,256,256]{3,2,1,0:T(8,128)(2,1)} %w_hbm.1, f32[2,4096]{1,0:T(2,128)} %bias_hbm.1, f32[1,4096]{1,0:T(1,128)} %bitcast.7), custom_call_target="tpu_custom_call" | custom-call | tf_op jit(solution)/shard_map/pallas_call | solution.py:755
  65.4 2.2 %shard_map.85 = (bf16[128,4096]{1,0:T(8,128)(2,1)}, f32[32,256]{1,0:T(8,128)}, f32[2,4096]{1,0:T(2,128)}, f32[1,4096]{1,0:T(1,128)}) custom-call(bf16[128,4096]{1,0:T(8,128)(2,1)} %get-tuple-element.12.refs_0_, f32[32,256]{1,0:T(8,128)} %get-tuple-element.13.refs_1_, f32[2,4096]{1,0:T(2,128)} %get-tuple-element.14.refs_2_, f32[1,4096]{1,0:T(1,128)} %get-tuple-element.15.refs_3_), custom_call_target="tpu_custom_call" | custom-call | tf_op jit(solution)/shard_map/pallas_call | solution.py:768
